TPU v7x, 256 devices: a whole 4x4x8 slice. The times are simulated.
256 devices in a mesh: row: 32 (over y, x, core), col: 8 (over z).
Axes of the slice: x: 4, y: 4, z: 8, core: 2. Of those that a mesh axis runs over, the one named last changes fastest.
Arguments:
- grad: bfloat16 [8192, 26624], P('row', 'col'), may hold values from -6 to 6
- momentum: bfloat16 [8192, 26624], P('row', 'col'), may hold values from -6 to 6
- q_prev: float32 [26624, 128], P('col'), may hold values from -0.0390625 to 0.0390625
Outputs:
- momentum_new: bfloat16 [8192, 26624], P('row', 'col')
- direction: bfloat16 [8192, 26624], P('row', 'col')
- q_new: float32 [26624, 128], P('col')
All inputs are finite; a program needn't handle non-finite values.
Results may differ from a plain program's by a relative error of at most 0.009.
Values may be sent and summed in bfloat16 or wider, within the bound.
A program may use at most 64 MiB of HBM per device.

v0:
```python
import math

import jax
import jax.numpy as jnp
from jax import lax
from jax.sharding import PartitionSpec as P

momentum_keep = 0.9
epsilon = 1e-06


def orthonormal(power, gram_matrix):
    lower = jnp.linalg.cholesky(gram_matrix)
    solved = lax.linalg.triangular_solve(
        lower, power, left_side=False, lower=True, transpose_a=True
    )
    return solved.astype(jnp.bfloat16)


def per_device(grad, momentum, q_prev):
    buffer = momentum_keep * momentum.astype(jnp.float32) + grad.astype(jnp.float32)
    buffer_b = buffer.astype(jnp.bfloat16)
    q_b = q_prev.astype(jnp.bfloat16)
    local_rows = buffer_b.shape[0]
    local_cols = buffer_b.shape[1]
    partial_power = jnp.dot(buffer_b, q_b, preferred_element_type=jnp.float32)
    power = lax.psum(partial_power, "col")
    gram_matrix = lax.psum(jnp.dot(power.T, power, precision=lax.Precision.HIGHEST), "row")
    ortho_b = orthonormal(power, gram_matrix)
    partial_factor = jnp.einsum("ij,ik->jk", buffer_b, ortho_b, preferred_element_type=jnp.float32)
    factor = lax.psum(partial_factor, "row")
    squares = lax.psum(jnp.sum(factor * factor, axis=0), "col")
    q_new = factor / jnp.sqrt(squares + epsilon)
    factor_b = factor.astype(jnp.bfloat16)
    feedback = jnp.dot(ortho_b, factor_b.T, preferred_element_type=jnp.float32)
    momentum_new = (buffer - (1.0 - momentum_keep) * feedback).astype(jnp.bfloat16)
    total_rows = local_rows * lax.axis_size("row")
    total_cols = local_cols * lax.axis_size("col")
    scaling = math.sqrt(total_rows * total_cols / q_prev.shape[1])
    update = jnp.dot(ortho_b, q_new.astype(jnp.bfloat16).T, preferred_element_type=jnp.float32)
    direction = (scaling * update).astype(jnp.bfloat16)
    return (momentum_new, direction, q_new)


def solution(mesh):
    return jax.shard_map(
        per_device,
        mesh=mesh,
        in_specs=(P("row", "col"), P("row", "col"), P("col", None)),
        out_specs=(P("row", "col"), P("row", "col"), P("col", None)),
        check_vma=False,
    )
```

profile of v0, /device:TPU:1, one launch (start us, length us, event | category | flops | bytes accessed | tf_op | source)
XLA Modules:
  0.0 367.4 jit_solution(603962532280243005)
XLA Ops:
  7.2 0.0 all-reduce.4.cloned.1.call-start
  7.2 0.0 copy-start
  7.2 0.0 copy-start.1
  7.2 4.0 %fusion.6 = f32[256,128]{1,0:T(8,128)} fusion(f32[3328,128]{1,0:T(8,128)} %param.5, bf16[256,3328]{1,0:T(8,128)(2,1)} %param.3, bf16[256,3328]{1,0:T(8,128)(2,1)} %param.4), kind=kOutput, calls=%fused_computation.12 | convolution fusion | flops 222789632 | bytes 5242880 | tf_op jit(solution)/shard_map/dot_general | solution.py:26
  11.3 0.0 all-reduce.4.cloned.1.call-update
  11.3 0.0 all-reduce.6.cloned.1.call-start
  11.3 70.8 %all-reduce.4.cloned.1.call-done = f32[256,128]{1,0:T(8,128)} async-done(((f32[256,128]{1,0:T(8,128)}), f32[256,128]{1,0:T(8,128)}) %all-reduce.4.cloned.1.call-update) | async-done | bytes 131088 | tf_op jit(solution)/shard_map/psum | solution.py:27
  82.1 2.0 fusion.16
  84.1 0.0 all-reduce.6.cloned.1.call-update
  84.1 0.0 all-reduce.8.cloned.1.call-start
  84.2 111.6 %all-reduce.6.cloned.1.call-done = f32[128,128]{0,1:T(8,128)} async-done(((f32[128,128]{0,1:T(8,128)}), f32[128,128]{0,1:T(8,128)}) %all-reduce.6.cloned.1.call-update) | async-done | bytes 65552 | tf_op jit(solution)/shard_map/psum | solution.py:28
  195.8 0.9 copy.7
  196.7 0.9 fusion.13
  197.6 11.7 %cholesky.16 = f32[128,128]{1,0:T(8,128)S(1)} custom-call(f32[128,128]{1,0:T(8,128)S(1)} %fusion.13), custom_call_target="Cholesky" | custom-call | tf_op jit(solution)/shard_map/jit(cholesky)/cholesky | solution.py:13
  209.3 0.6 compare_reduce_fusion
  210.0 0.7 fusion.11
  210.6 10.4 %custom-call.6 = f32[1,128,128]{1,2,0:T(8,128)} custom-call(f32[1,128,128]{2,1,0:T(8,128)S(1)} %fusion.11), custom_call_target="InvertDiagBlocksLowerTriangular" | custom-call | tf_op jit(solution)/shard_map/triangular_solve | solution.py:14
  221.1 1.2 convolution_convert_fusion
  222.2 0.0 copy-done
  222.3 0.0 copy-done.1
  222.3 1.9 fusion.8
  224.2 0.0 all-reduce.8.cloned.1.call-update
  224.2 114.7 %all-reduce.8.cloned.1.call-done = f32[3328,128]{1,0:T(8,128)} async-done(((f32[3328,128]{1,0:T(8,128)}), f32[3328,128]{1,0:T(8,128)}) %all-reduce.8.cloned.1.call-update) | async-done | bytes 1703952 | tf_op jit(solution)/shard_map/psum | solution.py:31
  338.9 1.9 multiply_reduce_fusion
  340.8 13.7 %psum.31 = f32[128]{0:T(128)S(1)} all-reduce(f32[128]{0:T(128)S(1)} %multiply_reduce_fusion), channel_id=1, replica_groups=mesh['row'=32,'col'=8] {'col'}, use_global_device_ids=true, to_apply=%region_6.7 | all-reduce | flops 128 | bytes 1024 | tf_op jit(solution)/shard_map/psum | solution.py:32
  354.5 1.6 broadcast_divide_fusion
  356.1 0.0 copy-start.3
  356.1 0.0 copy-start.2
  356.1 1.8 fusion.2
  357.9 0.0 copy-done.3
  357.9 0.9 copy-done.2
  358.8 2.1 fusion.1
  (2 shorter events, 0.0 us)
Async XLA Ops:
  7.2 75.0 %all-reduce.4.cloned.1.call-start = ((), (), s32[]{:S(2)}) async-start(), calls=%async_computation | async-start | bytes 262144 | tf_op jit(solution)/shard_map/psum | solution.py:27
  7.2 215.0 %copy-start = (bf16[256,3328]{1,0:T(8,128)(2,1)S(1)}, bf16[256,3328]{1,0:T(8,128)(2,1)}, u32[]{:S(2)}) copy-start(bf16[256,3328]{1,0:T(8,128)(2,1)} %param.3) | copy-start | bytes 5111812
  7.2 215.0 %copy-start.1 = (bf16[256,3328]{1,0:T(8,128)(2,1)S(1)}, bf16[256,3328]{1,0:T(8,128)(2,1)}, u32[]{:S(2)}) copy-start(bf16[256,3328]{1,0:T(8,128)(2,1)} %param.4) | copy-start | bytes 5111812
  11.3 184.5 %all-reduce.6.cloned.1.call-start = ((), (), s32[]{:S(2)}) async-start(), calls=%async_computation.1 | async-start | bytes 131072 | tf_op jit(solution)/shard_map/psum | solution.py:28
  84.1 254.7 %all-reduce.8.cloned.1.call-start = ((), (), s32[]{:S(2)}) async-start(), calls=%async_computation.2 | async-start | bytes 3407872 | tf_op jit(solution)/shard_map/psum | solution.py:31
  356.1 1.8 copy-start.3
  356.1 2.7 copy-start.2
Sparse Core Ops, SparseCore 0:
  11.4 70.6 all-reduce.3
  86.3 109.4 all-reduce.5
  224.3 114.5 all-reduce.7
where the time goes:
time: 372 us; the launch traced here: 367 us
  waiting for transfers between devices  297 us (80%)
  other arithmetic  27.8 us (7%)
  between operations  13.8 us (4%)
  blocking collectives  13.7 us (4%)
  matrix products  13 us (3%)
    psum x1, waiting for transfers between devices, per_device(): factor = lax.psum(partial_factor, 'row')  115 us
    psum x1, waiting for transfers between devices, per_device(): lax.psum(jnp.dot(power.T, power, precision=lax.Precision.HIGHEST), 'row')  112 us
    psum x1, waiting for transfers between devices, per_device(): power = lax.psum(partial_power, 'col')  70.8 us
    psum x1, blocking collectives, per_device(): squares = lax.psum(jnp.sum(factor * factor, axis=0), 'col')  13.7 us
    another operation x3, other arithmetic, orthonormal(): lower = jnp.linalg.cholesky(gram_matrix)  12.4 us
    another operation x2, other arithmetic, orthonormal(): lax.linalg.triangular_solve(lower, power, left_side=False, lower=True, tr...  11.1 us
  transfers between devices with their start and end apart: 3, of which 3 were waited for; matrix products, arithmetic and copies ran while one was open for 0% of the time, Pallas kernels for 0%

commit v1 on v0

v1 whole, which is shorter than its diff:
```python
import functools
import math

import jax
import jax.numpy as jnp
from jax import lax
from jax.experimental import pallas as pl
from jax.experimental.pallas import tpu as pltpu
from jax.sharding import PartitionSpec as P

momentum_keep = 0.9
epsilon = 1e-06
MESH = pl.DeviceIdType.MESH
HIGHEST = lax.Precision.HIGHEST
LANES = 128
Z = 8
CHIPS = 16


def remote(src, dst, send, recv, device):
    return pltpu.make_async_remote_copy(
        src_ref=src, dst_ref=dst, send_sem=send, recv_sem=recv, device_id=device, device_id_type=MESH
    )


def inverse_cholesky(a_ref):
    rank = a_ref.shape[0]
    lane = lax.broadcasted_iota(jnp.int32, (8, LANES), 1)
    sub = lax.broadcasted_iota(jnp.int32, (8, LANES), 0)
    lane_all = lax.broadcasted_iota(jnp.int32, (rank, LANES), 1)
    row_all = lax.broadcasted_iota(jnp.int32, (rank, LANES), 0)

    def block(b, _):
        rows = pl.ds(pl.multiple_of(b * 8, 8), 8)
        a = a_ref[...]
        r = a_ref[rows, :]
        cols = [jnp.broadcast_to(r[:, k : k + 1], (8, LANES)) for k in range(8)]
        q = jnp.where(lane < 8, 0.0, r)
        v = jnp.zeros((8, LANES), jnp.float32)
        pivots = jnp.zeros((8, LANES), jnp.float32)
        inverses = jnp.zeros((8, LANES), jnp.float32)
        for j in range(8):
            pivot = jnp.broadcast_to(cols[j][j : j + 1, :], (8, LANES))
            inv = 1.0 / pivot
            here = sub == j
            m = jnp.where(here, 0.0, cols[j] * inv)
            qj = jnp.broadcast_to(q[j : j + 1, :], (8, LANES)) + jnp.where(lane == j, 1.0, 0.0)
            pivots = jnp.where(here, pivot, pivots)
            inverses = jnp.where(here, inv, inverses)
            v = jnp.where(here, qj, v)
            q = jnp.where(here, qj, q - m * qj)
            for k in range(j + 1, 8):
                cols[k] = cols[k] - m * jnp.broadcast_to(cols[k][j : j + 1, :], (8, LANES))
        q = q * inverses
        new = jnp.where(lane_all < 8, 0.0, a)
        below = row_all >= b * 8 + 8
        total = jnp.zeros((rank, LANES), jnp.float32)
        for k in range(8):
            total = total + a[:, k : k + 1] * q[k : k + 1, :]
        new = jnp.where(below, new - total, new)
        a_ref[...] = pltpu.roll(new, LANES - 8, 1)
        a_ref[rows, :] = pltpu.roll(v * lax.rsqrt(pivots), LANES - 8, 1)
        return 0

    lax.fori_loop(0, rank // 8, block, 0)


NEAR = sorted(
    ((dy, dx) for dy in range(4) for dx in range(4) if (dy, dx) != (0, 0)),
    key=lambda d: min(d[0], 4 - d[0]) + min(d[1], 4 - d[1]),
)


def main_kernel(
    grad, mom, qprev, factor, ortho, sq, mnew,
    gbuf, mbuf, qbuf, buf, bb, pp, prs, pw, p3, pk, cg, gx, gs, amat, wt, wc, wr, fb, sz, sx, sc,
    in_sem, s1, r1, s2, r2, s3, r3, s4, r4, s5, r5, s6, r6, s7, r7, s8, r8, s9, r9, sf, s10, r10, s11, r11,
):
    rowi = lax.axis_index("row")
    c = lax.axis_index("col")
    chip = rowi // 2
    k = lax.rem(rowi, 2)
    other = 1 - k
    sibling = (chip * 2 + other, c)
    tiles = bb.shape[1] // LANES
    share = wr.shape[1]

    def zpeer(o):
        t = lax.rem(c + o, Z)
        return t, (rowi, t)

    def cpeer(d):
        t = lax.rem(chip // 4 + d[0], 4) * 4 + lax.rem(chip + d[1], 4)
        return t, (t * 2 + k, c)

    others = [cpeer(d) for d in NEAR]

    bounds = [0, 7, 14, 20, tiles]
    loads = []
    for i in range(4):
        lanes = pl.ds(bounds[i] * LANES, (bounds[i + 1] - bounds[i]) * LANES)
        part = [
            pltpu.make_async_copy(grad.at[:, lanes], gbuf.at[:, lanes], in_sem.at[i, 0]),
            pltpu.make_async_copy(mom.at[:, lanes], mbuf.at[:, lanes], in_sem.at[i, 1]),
            pltpu.make_async_copy(qprev.at[lanes, :], qbuf.at[lanes, :], in_sem.at[i, 2]),
        ]
        for copy in part:
            copy.start()
        loads.append(part)

    barrier = pltpu.get_barrier_semaphore()

    for o in range(1, Z):
        pl.semaphore_signal(barrier, inc=1, device_id=zpeer(o)[1], device_id_type=MESH)
    for _, dev in others:
        pl.semaphore_signal(barrier, inc=1, device_id=dev, device_id_type=MESH)
    pl.semaphore_signal(barrier, inc=1, device_id=sibling, device_id_type=MESH)

    rows = bb.shape[0]
    for i in range(4):
        for copy in loads[i]:
            copy.wait()
        lanes = pl.ds(bounds[i] * LANES, (bounds[i + 1] - bounds[i]) * LANES)

        def strip(s, _):
            rs = pl.ds(pl.multiple_of(s * 32, 32), 32)
            g = gbuf[rs, lanes].astype(jnp.float32)
            m = mbuf[rs, lanes].astype(jnp.float32)
            b = momentum_keep * m + g
            buf[rs, lanes] = b
            bb[rs, lanes] = b.astype(jnp.bfloat16)
            return 0

        lax.fori_loop(0, rows // 32, strip, 0)
        d = jnp.dot(bb[:, lanes], qbuf[lanes, :].astype(jnp.bfloat16), preferred_element_type=jnp.float32)
        d = d.reshape(Z, rows // Z, LANES)
        pp[...] = d if i == 0 else pp[...] + d

    pl.semaphore_wait(barrier, Z - 1 + CHIPS - 1 + 1)

    far_first = (4, 3, 5, 2, 6, 1, 7)
    sends = []
    for o in far_first:
        t, dev = zpeer(o)
        copy = remote(pp.at[t], prs.at[c], s1.at[o], r1.at[c], dev)
        copy.start()
        sends.append(copy)
    red = pp[c]
    for o in (1, 7, 2, 6, 3, 5, 4):
        s = lax.rem(c + o, Z)
        remote(pp.at[s], prs.at[s], s1.at[0], r1.at[s], sibling).wait_recv()
        red = red + prs[s]
    pw[c] = red
    for o in far_first:
        t, dev = zpeer(o)
        copy = remote(pw.at[c], pw.at[c], s2.at[o], r2.at[c], dev)
        copy.start()
        sends.append(copy)
    for o in (1, 7, 2, 6, 3, 5, 4):
        s = lax.rem(c + o, Z)
        remote(pw.at[s], pw.at[s], s2.at[0], r2.at[s], sibling).wait_recv()

    power = pw[...].reshape(rows, LANES)
    pt = power.T
    gram = jnp.dot(pt, power, precision=HIGHEST, preferred_element_type=jnp.float32)
    lane64 = lax.broadcasted_iota(jnp.int32, (64, LANES), 1)
    lane32 = lax.broadcasted_iota(jnp.int32, (32, LANES), 1)
    top, bottom = gram[:64], gram[64:]
    pk[0:64] = jnp.where(lane64 < 64, top, bottom)
    pk[64:96] = jnp.where(lane32 >= 64, top[:32], pltpu.roll(top[32:], 64, 1))
    mine = pl.ds(pl.multiple_of(k * 48, 16), 48)
    theirs = pl.ds(pl.multiple_of(other * 48, 16), 48)
    copy = remote(pk.at[theirs], cg, s3, r3, sibling)
    copy.start()
    sends.append(copy)

    hi = power.astype(jnp.bfloat16)
    rest = power - hi.astype(jnp.float32)
    mid = rest.astype(jnp.bfloat16)
    p3[:, 0:128] = hi
    p3[:, 128:256] = mid
    p3[:, 256:384] = (rest - mid.astype(jnp.float32)).astype(jnp.bfloat16)
    for i in range(4):
        cols = slice(bounds[i] * LANES, bounds[i + 1] * LANES)
        d = lax.dot_general(bb[:, cols], p3[...], (((0,), (0,)), ((), ())), preferred_element_type=jnp.float32)
        wt[cols, :] = d[:, 0:128] + (d[:, 128:256] + d[:, 256:384])

    def shares(u, core):
        return wt.at[pl.ds(pl.multiple_of((2 * u + core) * share, 8), share)]

    def exchange(u):
        return remote(shares(u, other), wc.at[u], s4.at[u], r4.at[u], sibling)

    for u, _ in others:
        exchange(u).start()
    exchange(chip).start()

    remote(cg, cg, s3, r3, sibling).wait_recv()
    gx[chip] = pk[mine] + cg[...]
    for i, (t, dev) in enumerate(others):
        copy = remote(gx.at[chip], gx.at[chip], s5.at[i], r5.at[chip], dev)
        copy.start()
        sends.append(copy)

    for i, (u, dev) in enumerate(others):
        exchange(u).wait_recv()
        wc[u] = wc[u] + shares(u, k)[...]
        copy = remote(wc.at[u], wr.at[chip], s6.at[i], r6.at[chip], dev)
        copy.start()
        sends.append(copy)
    exchange(chip).wait_recv()
    wr[chip] = wc[chip] + shares(chip, k)[...]

    for s, _ in others:
        remote(gx.at[s], gx.at[s], s5.at[0], r5.at[s], sibling).wait_recv()
    total = gx[0]
    for s in range(1, CHIPS):
        total = total + gx[s]
    gs[mine] = total
    copy = remote(gs.at[mine], gs.at[mine], s7, r7, sibling)
    copy.start()
    sends.append(copy)
    remote(gs.at[theirs], gs.at[theirs], s7, r7, sibling).wait_recv()
    ga = gs[0:64]
    gb = gs[64:96]
    upper = jnp.concatenate([gb, pltpu.roll(gb, 64, 1)], axis=0)
    top = jnp.where(lane64 < 64, ga, upper)
    low = top.T[64:]
    amat[0:64] = top
    amat[64:128] = jnp.where(lane64 < 64, jnp.concatenate([low, low], axis=1), ga)

    inverse_cholesky(amat)
    linv = amat[...]

    slot = chip * 2 + k
    for s, _ in others:
        remote(wr.at[s], wr.at[s], s6.at[0], r6.at[s], sibling).wait_recv()
    w = wr[0]
    for s in range(1, CHIPS):
        w = w + wr[s]
    f = lax.dot_general(w, linv, (((1,), (1,)), ((), ())), precision=HIGHEST, preferred_element_type=jnp.float32)
    sz[c] = jnp.broadcast_to(jnp.sum(f * f, axis=0, keepdims=True), (8, LANES))
    for o in far_first:
        t, dev = zpeer(o)
        copy = remote(sz.at[c], sz.at[c], s9.at[o], r9.at[c], dev)
        copy.start()
        sends.append(copy)
    fb[slot] = jnp.concatenate([f, jnp.zeros((fb.shape[1] - share, LANES), jnp.float32)], axis=0).astype(jnp.bfloat16)
    for i, (t, dev) in enumerate(others):
        copy = remote(fb.at[slot], fb.at[slot], s8.at[i], r8.at[slot], dev)
        copy.start()
        sends.append(copy)

    def forward(t):
        place = t * 2 + k
        return remote(fb.at[place], fb.at[place], sf.at[t], r8.at[place], sibling)

    forward(chip).start()
    ortho[...] = lax.dot_general(
        pw[...].reshape(rows, LANES), linv, (((1,), (1,)), ((), ())), precision=HIGHEST, preferred_element_type=jnp.float32
    ).astype(jnp.bfloat16)
    for o in (1, 7, 2, 6, 3, 5, 4):
        s = lax.rem(c + o, Z)
        remote(sz.at[s], sz.at[s], s9.at[0], r9.at[s], sibling).wait_recv()
    tot = sz[0]
    for s in range(1, Z):
        tot = tot + sz[s]
    sx[chip] = tot

    for i, (t, dev) in enumerate(others):
        copy = remote(sx.at[chip], sx.at[chip], s10.at[i], r10.at[chip], dev)
        copy.start()
        sends.append(copy)

    for t, _ in others:
        forward(t).wait_recv()
        forward(t).start()
    for s, _ in others:
        remote(sx.at[s], sx.at[s], s10.at[0], r10.at[s], sibling).wait_recv()
    tot = sx[0]
    for s in range(1, CHIPS):
        tot = tot + sx[s]
    sc[k] = tot
    copy = remote(sc.at[k], sc.at[k], s11, r11, sibling)
    copy.start()
    sends.append(copy)

    for t in range(CHIPS):
        place = t * 2 + other
        remote(fb.at[place], fb.at[place], sf.at[t], r8.at[place], sibling).wait_recv()
    for i in range(2 * CHIPS):
        factor[i * share : (i + 1) * share, :] = fb[i, 0:share].astype(jnp.float32)
    for t in range(tiles // 2):
        cols = slice(t * 2 * LANES, (t + 1) * 2 * LANES)
        d = lax.dot_general(
            ortho[...],
            factor[cols, :].astype(jnp.bfloat16),
            (((1,), (1,)), ((), ())),
            preferred_element_type=jnp.float32,
        )
        mnew[:, cols] = (buf[:, cols] - (1.0 - momentum_keep) * d).astype(jnp.bfloat16)

    remote(sc.at[other], sc.at[other], s11, r11, sibling).wait_recv()
    sq[...] = sc[0] + sc[1]

    for copy in sends:
        copy.wait_send()

    for t in range(CHIPS):
        exchange(t).wait_send()
        forward(t).wait_send()


def final_kernel(scaling, factor, ortho, sq, mnew, mout, direction, qnew, dbuf, qbuf, sem):
    copy = pltpu.make_async_copy(mnew, mout, sem.at[0, 0])
    copy.start()
    copies = [copy]
    inv = 1.0 / jnp.sqrt(sq[0:1] + epsilon)
    o = ortho[...]
    steps = factor.shape[0] // (2 * LANES)
    for part, (first, last) in enumerate(((0, 4), (4, 8), (8, steps))):
        for u in range(first, last):
            cols = slice(2 * u * LANES, 2 * (u + 1) * LANES)
            q = factor[cols, :] * inv
            qbuf[cols, :] = q
            update = lax.dot_general(
                o, q.astype(jnp.bfloat16), (((1,), (1,)), ((), ())), preferred_element_type=jnp.float32
            )
            dbuf[:, cols] = (scaling * update).astype(jnp.bfloat16)
        cols = pl.ds(first * 2 * LANES, (last - first) * 2 * LANES)
        for n, (src, dst) in enumerate(((dbuf.at[:, cols], direction.at[:, cols]), (qbuf.at[cols, :], qnew.at[cols, :]))):
            copy = pltpu.make_async_copy(src, dst, sem.at[1 + part, n])
            copy.start()
            copies.append(copy)
    for copy in copies:
        copy.wait()


def per_device(grad, momentum, q_prev):
    rows, cols = grad.shape
    share = cols // (2 * CHIPS)
    f32, bf16 = jnp.float32, jnp.bfloat16
    dma = pltpu.SemaphoreType.DMA
    vmem = pl.BlockSpec(memory_space=pltpu.VMEM)
    hbm = pl.BlockSpec(memory_space=pltpu.HBM)
    factor, ortho, sq, mnew = pl.pallas_call(
        main_kernel,
        out_shape=(
            jax.ShapeDtypeStruct((cols, LANES), f32),
            jax.ShapeDtypeStruct((rows, LANES), bf16),
            jax.ShapeDtypeStruct((8, LANES), f32),
            jax.ShapeDtypeStruct((rows, cols), bf16),
        ),
        in_specs=[hbm] * 3,
        out_specs=(vmem,) * 4,
        scratch_shapes=[
            pltpu.VMEM((rows, cols), bf16),
            pltpu.VMEM((rows, cols), bf16),
            pltpu.VMEM((cols, LANES), f32),
            pltpu.VMEM((rows, cols), f32),
            pltpu.VMEM((rows, cols), bf16),
            pltpu.VMEM((Z, rows // Z, LANES), f32),
            pltpu.VMEM((Z, rows // Z, LANES), f32),
            pltpu.VMEM((Z, rows // Z, LANES), f32),
            pltpu.VMEM((rows, 3 * LANES), bf16),
            pltpu.VMEM((96, LANES), f32),
            pltpu.VMEM((48, LANES), f32),
            pltpu.VMEM((CHIPS, 48, LANES), f32),
            pltpu.VMEM((96, LANES), f32),
            pltpu.VMEM((LANES, LANES), f32),
            pltpu.VMEM((cols, LANES), f32),
            pltpu.VMEM((CHIPS, share, LANES), f32),
            pltpu.VMEM((CHIPS, share, LANES), f32),
            pltpu.VMEM((2 * CHIPS, -(-share // 16) * 16, LANES), bf16),
            pltpu.VMEM((Z, 8, LANES), f32),
            pltpu.VMEM((CHIPS, 8, LANES), f32),
            pltpu.VMEM((2, 8, LANES), f32),
            dma((4, 3)),
            dma((Z,)), dma((Z,)),
            dma((Z,)), dma((Z,)),
            dma, dma,
            dma((CHIPS,)), dma((CHIPS,)),
            dma((CHIPS,)), dma((CHIPS,)),
            dma((CHIPS,)), dma((CHIPS,)),
            dma, dma,
            dma((CHIPS,)), dma((2 * CHIPS,)),
            dma((Z,)), dma((Z,)),
            dma((CHIPS,)),
            dma((CHIPS,)), dma((CHIPS,)),
            dma, dma,
        ],
        compiler_params=pltpu.CompilerParams(
            collective_id=0, has_side_effects=True, vmem_limit_bytes=40 * 2**20
        ),
        name="power_gram_factor",
    )(*(pltpu.with_memory_space_constraint(x, pltpu.HBM) for x in (grad, momentum, q_prev)))

    total_rows = rows * lax.axis_size("row")
    total_cols = cols * lax.axis_size("col")
    scaling = math.sqrt(total_rows * total_cols / q_prev.shape[1])
    return pl.pallas_call(
        functools.partial(final_kernel, scaling),
        out_shape=(
            jax.ShapeDtypeStruct((rows, cols), bf16),
            jax.ShapeDtypeStruct((rows, cols), bf16),
            jax.ShapeDtypeStruct((cols, LANES), f32),
        ),
        in_specs=[vmem] * 4,
        out_specs=(hbm,) * 3,
        scratch_shapes=[pltpu.VMEM((rows, cols), bf16), pltpu.VMEM((cols, LANES), f32), dma((4, 2))],
        compiler_params=pltpu.CompilerParams(vmem_limit_bytes=24 * 2**20),
        name="outputs",
    )(factor, ortho, sq, mnew)


def solution(mesh):
    return jax.shard_map(
        per_device,
        mesh=mesh,
        in_specs=(P("row", "col"), P("row", "col"), P("col", None)),
        out_specs=(P("row", "col"), P("row", "col"), P("col", None)),
        check_vma=False,
    )
```

time: 372 us -> 56.8 us (0.15); the launches traced: 367 us -> 56.7 us
  waiting for transfers between devices: 297 us -> 0 us
  Pallas kernels: 0 us -> 56.1 us
  other arithmetic: 27.8 us -> 0 us
  blocking collectives: 13.7 us -> 0 us
  between operations: 13.8 us -> 0.64 us
  matrix products: 13 us -> 0 us
    psum x3 -> x0, waiting for transfers between devices: 297 us -> none  [the longest x1 115 us: per_device(): factor = lax.psum(partial_factor, 'row')]
    pallas_call x0 -> x2, Pallas kernels: none -> 56.1 us  [the longest x1 53.7 us: per_device(): pl.pallas_call(main_kernel, out_shape=(jax.ShapeDtypeStruct((cols, LANES)...]
    another operation x5 -> x0, other arithmetic: 23.5 us -> none  [the longest x3 12.4 us: orthonormal(): lower = jnp.linalg.cholesky(gram_matrix)]
    psum x1 -> x0, blocking collectives: 13.7 us -> none  [per_device(): squares = lax.psum(jnp.sum(factor * factor, axis=0), 'col')]
    dot_general x5 -> x0, matrix products: 11.9 us -> none  [the longest x1 4.04 us: per_device(): partial_power = jnp.dot(buffer_b, q_b, preferred_element_type=jnp.float32)]
  transfers between devices with their start and end apart: 3 -> 0, of which waited for: 3 -> 0; matrix products, arithmetic and copies ran while one was open for 0% -> 0% of each run, Pallas kernels for 0% -> 0%
where the time goes in v1:
time: 56.8 us; the launch traced here: 56.7 us
  Pallas kernels  56.1 us (99%)
  between operations  0.64 us (1%)
    pallas_call x1, Pallas kernels, per_device(): pl.pallas_call(main_kernel, out_shape=(jax.ShapeDtypeStruct((cols, LANES)...  53.7 us
    pallas_call x1, Pallas kernels, per_device(): pl.pallas_call(functools.partial(final_kernel, scaling), out_shape=(jax.S...  2.37 us

profile of v1, /device:TPU:1, one launch (start us, length us, event | category | flops | bytes accessed | tf_op | source)
XLA Modules:
  0.0 56.7 jit_solution(8535260183714283705)
XLA Ops:
  0.6 53.7 %power_gram_factor.1 = (f32[3328,128]{1,0:T(8,128)S(1)}, bf16[256,128]{1,0:T(8,128)(2,1)S(1)}, f32[8,128]{1,0:T(8,128)S(1)}, bf16[256,3328]{1,0:T(8,128)(2,1)S(1)}) custom-call(bf16[256,3328]{1,0:T(8,128)(2,1)} %grad.1, bf16[256,3328]{1,0:T(8,128)(2,1)} %mom.1, f32[3328,128]{1,0:T(8,128)} %qprev.1), custom_call_target="tpu_custom_call" | custom-call | tf_op jit(solution)/shard_map/power_gram_factor/pallas_call | solution.py:346
  54.3 2.4 %outputs.1 = (bf16[256,3328]{1,0:T(8,128)(2,1)}, bf16[256,3328]{1,0:T(8,128)(2,1)}, f32[3328,128]{1,0:T(8,128)}) custom-call(f32[3328,128]{1,0:T(8,128)S(1)} %get-tuple-element.7.factor, bf16[256,128]{1,0:T(8,128)(2,1)S(1)} %get-tuple-element.8.ortho, f32[8,128]{1,0:T(8,128)S(1)} %get-tuple-element.9.sq, bf16[256,3328]{1,0:T(8,128)(2,1)S(1)} %get-tuple-element.10.mnew), custom_call_target="tpu_custom_call" | custom-call | tf_op jit(solution)/shard_map/outputs/pallas_call | solution.py:401

commit v2 on v1

v2 whole, which is shorter than its diff:
```python
import functools
import math

import jax
import jax.numpy as jnp
from jax import lax
from jax.experimental import pallas as pl
from jax.experimental.pallas import tpu as pltpu
from jax.sharding import PartitionSpec as P

momentum_keep = 0.9
epsilon = 1e-06
MESH = pl.DeviceIdType.MESH
HIGHEST = lax.Precision.HIGHEST
LANES = 128
Z = 8
CHIPS = 16


def remote(src, dst, send, recv, device):
    return pltpu.make_async_remote_copy(
        src_ref=src, dst_ref=dst, send_sem=send, recv_sem=recv, device_id=device, device_id_type=MESH
    )


def inverse_cholesky(a_ref, out_ref):
    rank = a_ref.shape[0]
    size = 16
    lane = lax.broadcasted_iota(jnp.int32, (size, LANES), 1)
    sub = lax.broadcasted_iota(jnp.int32, (size, LANES), 0)

    def row(x, j):
        return jnp.broadcast_to(x[j : j + 1, :], (size, LANES))

    def blocks(first, last):
        low = first * size
        lane_all = lax.broadcasted_iota(jnp.int32, (rank - low, LANES), 1)

        def block(b, _):
            rows = pl.ds(pl.multiple_of(b * size, size), size)
            a = a_ref[low:rank, :]
            r = a_ref[rows, :]
            cols = [jnp.broadcast_to(r[:, k : k + 1], (size, LANES)) for k in range(size)]
            q = jnp.where(lane < size, 0.0, r)
            v = jnp.zeros((size, LANES), jnp.float32)
            pivots = jnp.zeros((size, LANES), jnp.float32)
            inverses = jnp.zeros((size, LANES), jnp.float32)
            for j in range(size):
                pivot = row(cols[j], j)
                inv = 1.0 / pivot
                here = sub == j
                m = jnp.where(here, 0.0, cols[j] * inv)
                qj = row(q, j) + jnp.where(lane == j, 1.0, 0.0)
                pivots = jnp.where(here, pivot, pivots)
                inverses = jnp.where(here, inv, inverses)
                v = jnp.where(here, qj, v)
                q = jnp.where(here, qj, q - m * qj)
                for k in range(j + 1, size):
                    cols[k] = cols[k] - m * row(cols[k], j)
            q = q * inverses
            total = jnp.zeros((rank - low, LANES), jnp.float32)
            for k in range(size):
                total = total + a[:, k : k + 1] * q[k : k + 1, :]
            a_ref[low:rank, :] = pltpu.roll(jnp.where(lane_all < size, 0.0, a) - total, LANES - size, 1)
            v = pltpu.roll(v * lax.rsqrt(pivots), b * size, 1)
            out_ref[rows, :] = jnp.where(lane < (b + 1) * size, v, 0.0)
            return 0

        lax.fori_loop(first, last, block, 0)

    quarter = rank // size // 4
    for i in range(4):
        blocks(i * quarter, (i + 1) * quarter)


FAR = [(dy, dx) for dy in (2, 1, 3, 0) for dx in (2, 1, 3, 0) if (dy, dx) != (0, 0)]
NEAR = sorted(FAR, key=lambda d: min(d[0], 4 - d[0]) + min(d[1], 4 - d[1]))
W_ORDER, G_ORDER, F_ORDER, S_ORDER = NEAR, FAR, FAR, FAR


def main_kernel(
    grad, mom, qprev, factor, ortho, sq, mnew,
    gbuf, mbuf, qbuf, buf, bb, pp, prs, pw, pt, p2, gh, cg, gx, gs, amat, lmat, wt, wc, wr, fb, sz, sx,
    in_sem, s1, r1, s2, r2, s3, r3, s4, r4, s5, r5, s6, r6, s7, r7, s8, r8, s9, r9, sf, s10, r10,
):
    rowi = lax.axis_index("row")
    c = lax.axis_index("col")
    chip = rowi // 2
    k = lax.rem(rowi, 2)
    other = 1 - k
    sibling = (chip * 2 + other, c)
    tiles = bb.shape[1] // LANES
    share = wr.shape[1]

    def zpeer(o):
        t = lax.rem(c + o, Z)
        return t, (rowi, t)

    def zother(o):
        return (chip * 2 + other, lax.rem(c + o, Z))

    def cpeer(d):
        t = lax.rem(chip // 4 + d[0], 4) * 4 + lax.rem(chip + d[1], 4)
        return t, (t * 2 + k, c)

    others = [cpeer(d) for d in NEAR]
    w_others = [cpeer(d) for d in W_ORDER]
    g_others = [cpeer(d) for d in G_ORDER]
    f_others = [cpeer(d) for d in F_ORDER]
    s_others = [cpeer(d) for d in S_ORDER]

    far_first = (4, 3, 5, 2, 6, 1, 7)
    barrier = pltpu.get_barrier_semaphore()

    for o in far_first:
        pl.semaphore_signal(barrier, inc=1, device_id=zpeer(o)[1], device_id_type=MESH)
    for o in far_first:
        pl.semaphore_signal(barrier, inc=1, device_id=zother(o), device_id_type=MESH)
    for _, dev in others:
        pl.semaphore_signal(barrier, inc=1, device_id=dev, device_id_type=MESH)
    pl.semaphore_signal(barrier, inc=1, device_id=sibling, device_id_type=MESH)

    bounds = [0, 7, 14, 20, tiles]
    loads = []
    for i in range(4):
        lanes = pl.ds(bounds[i] * LANES, (bounds[i + 1] - bounds[i]) * LANES)
        part = [
            pltpu.make_async_copy(grad.at[:, lanes], gbuf.at[:, lanes], in_sem.at[i, 0]),
            pltpu.make_async_copy(mom.at[:, lanes], mbuf.at[:, lanes], in_sem.at[i, 1]),
            pltpu.make_async_copy(qprev.at[lanes, :], qbuf.at[lanes, :], in_sem.at[i, 2]),
        ]
        for copy in part:
            copy.start()
        loads.append(part)

    rows = bb.shape[0]
    for i in range(4):
        for copy in loads[i]:
            copy.wait()
        lanes = pl.ds(bounds[i] * LANES, (bounds[i + 1] - bounds[i]) * LANES)

        def strip(s, _):
            rs = pl.ds(pl.multiple_of(s * 32, 32), 32)
            g = gbuf[rs, lanes].astype(jnp.float32)
            m = mbuf[rs, lanes].astype(jnp.float32)
            b = momentum_keep * m + g
            buf[rs, lanes] = b
            bb[rs, lanes] = b.astype(jnp.bfloat16)
            return 0

        lax.fori_loop(0, rows // 32, strip, 0)
        d = jnp.dot(bb[:, lanes], qbuf[lanes, :].astype(jnp.bfloat16), preferred_element_type=jnp.float32)
        d = d.reshape(Z, rows // Z, LANES)
        pp[...] = d if i == 0 else pp[...] + d

    pl.semaphore_wait(barrier, 2 * (Z - 1) + CHIPS - 1 + 1)

    sends = []
    for o in far_first:
        t, dev = zpeer(o)
        copy = remote(pp.at[t], prs.at[c], s1.at[o], r1.at[c], dev)
        copy.start()
        sends.append(copy)
    red = pp[c]
    for o in (1, 7, 2, 6, 3, 5, 4):
        s = lax.rem(c + o, Z)
        remote(pp.at[s], prs.at[s], s1.at[0], r1.at[s], sibling).wait_recv()
        red = red + prs[s]
    pw[c] = red
    for o in far_first:
        t, dev = zpeer(o)
        copy = remote(pw.at[c], pw.at[c], s2.at[o], r2.at[c], dev)
        copy.start()
        sends.append(copy)
    for o in (1, 7, 2, 6, 3, 5, 4):
        s = lax.rem(c + o, Z)
        remote(pw.at[s], pw.at[s], s2.at[0], r2.at[s], sibling).wait_recv()

    power = pw[...].reshape(rows, LANES)
    hi = power.astype(jnp.bfloat16)
    p2[:, 0:128] = hi
    p2[:, 128:256] = (power - hi.astype(jnp.float32)).astype(jnp.bfloat16)
    for i in range(4):
        start, stop = bounds[i] * LANES, bounds[i + 1] * LANES
        d = lax.dot_general(
            bb[:, start:stop], p2[...], (((0,), (0,)), ((), ())), preferred_element_type=jnp.float32
        )
        d = d[:, 0:128] + d[:, 128:256]
        for place in range(start // share, -(-stop // share)):
            a, b = max(start, place * share), min(stop, (place + 1) * share)
            wt[place // 2, place % 2, a - place * share : b - place * share, :] = d[a - start : b - start]

    def exchange(u):
        return remote(wt.at[u, other], wc.at[u], s4.at[u], r4.at[u], sibling)

    for u, _ in w_others:
        exchange(u).start()
    exchange(chip).start()

    pt[...] = power.T
    part = pt[pl.ds(pl.multiple_of(c * 16, 16), 16), :]
    part = jnp.dot(part, power, precision=HIGHEST, preferred_element_type=jnp.float32)
    gh[...] = part.reshape(2, 8, LANES)
    copy = remote(gh.at[other], cg, s3, r3, sibling)
    copy.start()
    sends.append(copy)

    remote(cg, cg, s3, r3, sibling).wait_recv()
    gx[chip] = gh[k] + cg[...]
    for i, (t, dev) in enumerate(g_others):
        copy = remote(gx.at[chip], gx.at[chip], s5.at[i], r5.at[chip], dev)
        copy.start()
        sends.append(copy)

    for i, (u, dev) in enumerate(w_others):
        exchange(u).wait_recv()
        wc[u] = wc[u] + wt[u, k]
        copy = remote(wc.at[u], wr.at[chip], s6.at[i], r6.at[chip], dev)
        copy.start()
        sends.append(copy)
    exchange(chip).wait_recv()
    wr[chip] = wc[chip] + wt[chip, k]

    for s, _ in others:
        remote(gx.at[s], gx.at[s], s5.at[0], r5.at[s], sibling).wait_recv()
    total = gx[0]
    for s in range(1, CHIPS):
        total = total + gx[s]
    eight = 2 * c + k

    def spread(ref, send, recv):
        for o in far_first:
            for core, dev in enumerate((zpeer(o)[1], zother(o))):
                copy = remote(ref.at[eight], ref.at[eight], send.at[core, o], recv.at[eight], dev)
                copy.start()
                sends.append(copy)
        copy = remote(ref.at[eight], ref.at[eight], send.at[0, 0], recv.at[eight], sibling)
        copy.start()
        sends.append(copy)

    def collect(ref, send, recv):
        for o in (0, 1, 7, 2, 6, 3, 5, 4):
            for core in (other,) if o == 0 else (k, other):
                s = 2 * lax.rem(c + o, Z) + core
                remote(ref.at[s], ref.at[s], send.at[0, 0], recv.at[s], sibling).wait_recv()

    gs[eight] = total
    spread(gs, s7, r7)
    collect(gs, s7, r7)
    amat[...] = gs[...].reshape(LANES, LANES)

    inverse_cholesky(amat, lmat)
    linv = lmat[...]

    slot = chip * 2 + k
    for s, _ in others:
        remote(wr.at[s], wr.at[s], s6.at[0], r6.at[s], sibling).wait_recv()
    w = wr[0]
    for s in range(1, CHIPS):
        w = w + wr[s]
    f = lax.dot_general(w, linv, (((1,), (1,)), ((), ())), precision=HIGHEST, preferred_element_type=jnp.float32)
    sz[eight] = jnp.broadcast_to(jnp.sum(f * f, axis=0, keepdims=True), (8, LANES))
    spread(sz, s9, r9)
    fb[slot] = jnp.concatenate([f, jnp.zeros((fb.shape[1] - share, LANES), jnp.float32)], axis=0).astype(jnp.bfloat16)
    for i, (t, dev) in enumerate(f_others):
        copy = remote(fb.at[slot], fb.at[slot], s8.at[i], r8.at[slot], dev)
        copy.start()
        sends.append(copy)

    def forward(t):
        place = t * 2 + k
        return remote(fb.at[place], fb.at[place], sf.at[t], r8.at[place], sibling)

    forward(chip).start()
    ortho[...] = lax.dot_general(
        pw[...].reshape(rows, LANES), linv, (((1,), (1,)), ((), ())), precision=HIGHEST, preferred_element_type=jnp.float32
    ).astype(jnp.bfloat16)
    collect(sz, s9, r9)
    tot = sz[0]
    for s in range(1, 2 * Z):
        tot = tot + sz[s]
    sx[chip] = tot

    for i, (t, dev) in enumerate(s_others):
        copy = remote(sx.at[chip], sx.at[chip], s10.at[i], r10.at[chip], dev)
        copy.start()
        sends.append(copy)

    for t, _ in f_others:
        forward(t).wait_recv()
        forward(t).start()
    for s, _ in others:
        remote(sx.at[s], sx.at[s], s10.at[0], r10.at[s], sibling).wait_recv()
    tot = sx[0]
    for s in range(1, CHIPS):
        tot = tot + sx[s]
    sq[...] = tot

    for t in range(CHIPS):
        place = t * 2 + other
        remote(fb.at[place], fb.at[place], sf.at[t], r8.at[place], sibling).wait_recv()
    for i in range(2 * CHIPS):
        factor[i * share : (i + 1) * share, :] = fb[i, 0:share].astype(jnp.float32)
    for t in range(tiles // 2):
        cols = slice(t * 2 * LANES, (t + 1) * 2 * LANES)
        d = lax.dot_general(
            ortho[...],
            factor[cols, :].astype(jnp.bfloat16),
            (((1,), (1,)), ((), ())),
            preferred_element_type=jnp.float32,
        )
        mnew[:, cols] = (buf[:, cols] - (1.0 - momentum_keep) * d).astype(jnp.bfloat16)

    for copy in sends:
        copy.wait_send()

    for t in range(CHIPS):
        exchange(t).wait_send()
        forward(t).wait_send()


def final_kernel(scaling, factor, ortho, sq, mnew, mout, direction, qnew, dbuf, qbuf, sem):
    copy = pltpu.make_async_copy(mnew, mout, sem.at[0, 0])
    copy.start()
    copies = [copy]
    inv = 1.0 / jnp.sqrt(sq[0:1] + epsilon)
    o = ortho[...]
    steps = factor.shape[0] // (2 * LANES)
    for part, (first, last) in enumerate(((0, 4), (4, 8), (8, steps))):
        for u in range(first, last):
            cols = slice(2 * u * LANES, 2 * (u + 1) * LANES)
            q = factor[cols, :] * inv
            qbuf[cols, :] = q
            update = lax.dot_general(
                o, q.astype(jnp.bfloat16), (((1,), (1,)), ((), ())), preferred_element_type=jnp.float32
            )
            dbuf[:, cols] = (scaling * update).astype(jnp.bfloat16)
        cols = pl.ds(first * 2 * LANES, (last - first) * 2 * LANES)
        for n, (src, dst) in enumerate(((dbuf.at[:, cols], direction.at[:, cols]), (qbuf.at[cols, :], qnew.at[cols, :]))):
            copy = pltpu.make_async_copy(src, dst, sem.at[1 + part, n])
            copy.start()
            copies.append(copy)
    for copy in copies:
        copy.wait()


def per_device(grad, momentum, q_prev):
    rows, cols = grad.shape
    share = cols // (2 * CHIPS)
    f32, bf16 = jnp.float32, jnp.bfloat16
    dma = pltpu.SemaphoreType.DMA
    vmem = pl.BlockSpec(memory_space=pltpu.VMEM)
    hbm = pl.BlockSpec(memory_space=pltpu.HBM)
    factor, ortho, sq, mnew = pl.pallas_call(
        main_kernel,
        out_shape=(
            jax.ShapeDtypeStruct((cols, LANES), f32),
            jax.ShapeDtypeStruct((rows, LANES), bf16),
            jax.ShapeDtypeStruct((8, LANES), f32),
            jax.ShapeDtypeStruct((rows, cols), bf16),
        ),
        in_specs=[hbm] * 3,
        out_specs=(vmem,) * 4,
        scratch_shapes=[
            pltpu.VMEM((rows, cols), bf16),
            pltpu.VMEM((rows, cols), bf16),
            pltpu.VMEM((cols, LANES), f32),
            pltpu.VMEM((rows, cols), f32),
            pltpu.VMEM((rows, cols), bf16),
            pltpu.VMEM((Z, rows // Z, LANES), f32),
            pltpu.VMEM((Z, rows // Z, LANES), f32),
            pltpu.VMEM((Z, rows // Z, LANES), f32),
            pltpu.VMEM((LANES, rows), f32),
            pltpu.VMEM((rows, 2 * LANES), bf16),
            pltpu.VMEM((2, 8, LANES), f32),
            pltpu.VMEM((8, LANES), f32),
            pltpu.VMEM((CHIPS, 8, LANES), f32),
            pltpu.VMEM((2 * Z, 8, LANES), f32),
            pltpu.VMEM((LANES, LANES), f32),
            pltpu.VMEM((LANES, LANES), f32),
            pltpu.VMEM((CHIPS, 2, share, LANES), f32),
            pltpu.VMEM((CHIPS, share, LANES), f32),
            pltpu.VMEM((CHIPS, share, LANES), f32),
            pltpu.VMEM((2 * CHIPS, -(-share // 16) * 16, LANES), bf16),
            pltpu.VMEM((2 * Z, 8, LANES), f32),
            pltpu.VMEM((CHIPS, 8, LANES), f32),
            dma((4, 3)),
            dma((Z,)), dma((Z,)),
            dma((Z,)), dma((Z,)),
            dma, dma,
            dma((CHIPS,)), dma((CHIPS,)),
            dma((CHIPS,)), dma((CHIPS,)),
            dma((CHIPS,)), dma((CHIPS,)),
            dma((2, Z)), dma((2 * Z,)),
            dma((CHIPS,)), dma((2 * CHIPS,)),
            dma((2, Z)), dma((2 * Z,)),
            dma((CHIPS,)),
            dma((CHIPS,)), dma((CHIPS,)),
        ],
        compiler_params=pltpu.CompilerParams(
            collective_id=0, has_side_effects=True, vmem_limit_bytes=40 * 2**20
        ),
        name="power_gram_factor",
    )(*(pltpu.with_memory_space_constraint(x, pltpu.HBM) for x in (grad, momentum, q_prev)))

    total_rows = rows * lax.axis_size("row")
    total_cols = cols * lax.axis_size("col")
    scaling = math.sqrt(total_rows * total_cols / q_prev.shape[1])
    return pl.pallas_call(
        functools.partial(final_kernel, scaling),
        out_shape=(
            jax.ShapeDtypeStruct((rows, cols), bf16),
            jax.ShapeDtypeStruct((rows, cols), bf16),
            jax.ShapeDtypeStruct((cols, LANES), f32),
        ),
        in_specs=[vmem] * 4,
        out_specs=(hbm,) * 3,
        scratch_shapes=[pltpu.VMEM((rows, cols), bf16), pltpu.VMEM((cols, LANES), f32), dma((4, 2))],
        compiler_params=pltpu.CompilerParams(vmem_limit_bytes=24 * 2**20),
        name="outputs",
    )(factor, ortho, sq, mnew)


def solution(mesh):
    return jax.shard_map(
        per_device,
        mesh=mesh,
        in_specs=(P("row", "col"), P("row", "col"), P("col", None)),
        out_specs=(P("row", "col"), P("row", "col"), P("col", None)),
        check_vma=False,
    )
```

time: 56.8 us -> 52.2 us (0.919)
  Pallas kernels: 56.1 us -> 51.5 us
    pallas_call x1, Pallas kernels: 53.7 us -> 49.2 us  [per_device(): pl.pallas_call(main_kernel, out_shape=(jax.ShapeDtypeStruct((cols, LANES)...]
where the time goes in v2:
time: 52.2 us
  Pallas kernels  51.5 us (99%)
  between operations  0.64 us (1%)
    pallas_call x1, Pallas kernels, per_device(): pl.pallas_call(main_kernel, out_shape=(jax.ShapeDtypeStruct((cols, LANES)...  49.2 us
    pallas_call x1, Pallas kernels, per_device(): pl.pallas_call(functools.partial(final_kernel, scaling), out_shape=(jax.S...  2.37 us

profile of v2, /device:TPU:1, one launch (start us, length us, event | category | flops | bytes accessed | tf_op | source)
XLA Modules:
  0.0 52.2 jit_solution(17307423465909886322)
XLA Ops:
  0.6 49.2 %power_gram_factor.1 = (f32[3328,128]{1,0:T(8,128)S(1)}, bf16[256,128]{1,0:T(8,128)(2,1)S(1)}, f32[8,128]{1,0:T(8,128)S(1)}, bf16[256,3328]{1,0:T(8,128)(2,1)S(1)}) custom-call(bf16[256,3328]{1,0:T(8,128)(2,1)} %grad.1, bf16[256,3328]{1,0:T(8,128)(2,1)} %mom.1, f32[3328,128]{1,0:T(8,128)} %qprev.1), custom_call_target="tpu_custom_call" | custom-call | tf_op jit(solution)/shard_map/power_gram_factor/pallas_call | solution.py:354
  49.8 2.4 %outputs.1 = (bf16[256,3328]{1,0:T(8,128)(2,1)}, bf16[256,3328]{1,0:T(8,128)(2,1)}, f32[3328,128]{1,0:T(8,128)}) custom-call(f32[3328,128]{1,0:T(8,128)S(1)} %get-tuple-element.7.factor, bf16[256,128]{1,0:T(8,128)(2,1)S(1)} %get-tuple-element.8.ortho, f32[8,128]{1,0:T(8,128)S(1)} %get-tuple-element.9.sq, bf16[256,3328]{1,0:T(8,128)(2,1)S(1)} %get-tuple-element.10.mnew), custom_call_target="tpu_custom_call" | custom-call | tf_op jit(solution)/shard_map/outputs/pallas_call | solution.py:409

commit v3 on v2

--- a/solution.py
+++ b/solution.py
@@ -79,8 +79,8 @@
 
 
 def main_kernel(
-    grad, mom, qprev, factor, ortho, sq, mnew,
-    gbuf, mbuf, qbuf, buf, bb, pp, prs, pw, pt, p2, gh, cg, gx, gs, amat, lmat, wt, wc, wr, fb, sz, sx,
+    grad, mom, qprev, factor, ortho, sq, buf,
+    gbuf, mbuf, qbuf, bb, pp, prs, pw, pt, p2, gh, cg, gx, gs, amat, lmat, wt, wc, wr, fb, sz, sx,
     in_sem, s1, r1, s2, r2, s3, r3, s4, r4, s5, r5, s6, r6, s7, r7, s8, r8, s9, r9, sf, s10, r10,
 ):
     rowi = lax.axis_index("row")
@@ -120,9 +120,9 @@
         pl.semaphore_signal(barrier, inc=1, device_id=dev, device_id_type=MESH)
     pl.semaphore_signal(barrier, inc=1, device_id=sibling, device_id_type=MESH)
 
-    bounds = [0, 7, 14, 20, tiles]
+    bounds = [0, 8, 15, 21, tiles - 2, tiles]
     loads = []
-    for i in range(4):
+    for i in range(5):
         lanes = pl.ds(bounds[i] * LANES, (bounds[i + 1] - bounds[i]) * LANES)
         part = [
             pltpu.make_async_copy(grad.at[:, lanes], gbuf.at[:, lanes], in_sem.at[i, 0]),
@@ -134,7 +134,7 @@
         loads.append(part)
 
     rows = bb.shape[0]
-    for i in range(4):
+    for i in range(5):
         for copy in loads[i]:
             copy.wait()
         lanes = pl.ds(bounds[i] * LANES, (bounds[i + 1] - bounds[i]) * LANES)
@@ -155,7 +155,13 @@
 
     pl.semaphore_wait(barrier, 2 * (Z - 1) + CHIPS - 1 + 1)
 
-    sends = []
+    sends, late = [], []
+
+    def drain(copies):
+        for copy in copies:
+            copy.wait_send()
+        copies.clear()
+
     for o in far_first:
         t, dev = zpeer(o)
         copy = remote(pp.at[t], prs.at[c], s1.at[o], r1.at[c], dev)
@@ -180,7 +186,7 @@
     hi = power.astype(jnp.bfloat16)
     p2[:, 0:128] = hi
     p2[:, 128:256] = (power - hi.astype(jnp.float32)).astype(jnp.bfloat16)
-    for i in range(4):
+    for i in range(5):
         start, stop = bounds[i] * LANES, bounds[i + 1] * LANES
         d = lax.dot_general(
             bb[:, start:stop], p2[...], (((0,), (0,)), ((), ())), preferred_element_type=jnp.float32
@@ -217,7 +223,7 @@
         wc[u] = wc[u] + wt[u, k]
         copy = remote(wc.at[u], wr.at[chip], s6.at[i], r6.at[chip], dev)
         copy.start()
-        sends.append(copy)
+        late.append(copy)
     exchange(chip).wait_recv()
     wr[chip] = wc[chip] + wt[chip, k]
 
@@ -228,7 +234,7 @@
         total = total + gx[s]
     eight = 2 * c + k
 
-    def spread(ref, send, recv):
+    def spread(ref, send, recv, sends):
         for o in far_first:
             for core, dev in enumerate((zpeer(o)[1], zother(o))):
                 copy = remote(ref.at[eight], ref.at[eight], send.at[core, o], recv.at[eight], dev)
@@ -245,7 +251,12 @@
                 remote(ref.at[s], ref.at[s], send.at[0, 0], recv.at[s], sibling).wait_recv()
 
     gs[eight] = total
-    spread(gs, s7, r7)
+    early = sends
+    sends = late
+    spread(gs, s7, r7, sends)
+    drain(early)
+    for t in range(CHIPS):
+        exchange(t).wait_send()
     collect(gs, s7, r7)
     amat[...] = gs[...].reshape(LANES, LANES)
 
@@ -260,12 +271,14 @@
         w = w + wr[s]
     f = lax.dot_general(w, linv, (((1,), (1,)), ((), ())), precision=HIGHEST, preferred_element_type=jnp.float32)
     sz[eight] = jnp.broadcast_to(jnp.sum(f * f, axis=0, keepdims=True), (8, LANES))
-    spread(sz, s9, r9)
+    early, sends = sends, []
+    spread(sz, s9, r9, sends)
     fb[slot] = jnp.concatenate([f, jnp.zeros((fb.shape[1] - share, LANES), jnp.float32)], axis=0).astype(jnp.bfloat16)
+    shared = []
     for i, (t, dev) in enumerate(f_others):
         copy = remote(fb.at[slot], fb.at[slot], s8.at[i], r8.at[slot], dev)
         copy.start()
-        sends.append(copy)
+        shared.append(copy)
 
     def forward(t):
         place = t * 2 + k
@@ -275,20 +288,24 @@
     ortho[...] = lax.dot_general(
         pw[...].reshape(rows, LANES), linv, (((1,), (1,)), ((), ())), precision=HIGHEST, preferred_element_type=jnp.float32
     ).astype(jnp.bfloat16)
+    drain(early)
     collect(sz, s9, r9)
     tot = sz[0]
     for s in range(1, 2 * Z):
         tot = tot + sz[s]
     sx[chip] = tot
 
+    last = []
     for i, (t, dev) in enumerate(s_others):
         copy = remote(sx.at[chip], sx.at[chip], s10.at[i], r10.at[chip], dev)
         copy.start()
-        sends.append(copy)
-
+        last.append(copy)
+
+    drain(sends)
     for t, _ in f_others:
         forward(t).wait_recv()
         forward(t).start()
+    drain(shared)
     for s, _ in others:
         remote(sx.at[s], sx.at[s], s10.at[0], r10.at[s], sibling).wait_recv()
     tot = sx[0]
@@ -301,43 +318,37 @@
         remote(fb.at[place], fb.at[place], sf.at[t], r8.at[place], sibling).wait_recv()
     for i in range(2 * CHIPS):
         factor[i * share : (i + 1) * share, :] = fb[i, 0:share].astype(jnp.float32)
-    for t in range(tiles // 2):
-        cols = slice(t * 2 * LANES, (t + 1) * 2 * LANES)
-        d = lax.dot_general(
-            ortho[...],
-            factor[cols, :].astype(jnp.bfloat16),
-            (((1,), (1,)), ((), ())),
-            preferred_element_type=jnp.float32,
-        )
-        mnew[:, cols] = (buf[:, cols] - (1.0 - momentum_keep) * d).astype(jnp.bfloat16)
-
-    for copy in sends:
-        copy.wait_send()
-
+    drain(last)
     for t in range(CHIPS):
-        exchange(t).wait_send()
         forward(t).wait_send()
 
 
-def final_kernel(scaling, factor, ortho, sq, mnew, mout, direction, qnew, dbuf, qbuf, sem):
-    copy = pltpu.make_async_copy(mnew, mout, sem.at[0, 0])
-    copy.start()
-    copies = [copy]
+def final_kernel(scaling, factor, ortho, sq, buf, mout, direction, qnew, mbuf, dbuf, qbuf, sem):
     inv = 1.0 / jnp.sqrt(sq[0:1] + epsilon)
     o = ortho[...]
     steps = factor.shape[0] // (2 * LANES)
-    for part, (first, last) in enumerate(((0, 4), (4, 8), (8, steps))):
+    copies = []
+
+    def times(x):
+        return lax.dot_general(
+            o, x.astype(jnp.bfloat16), (((1,), (1,)), ((), ())), preferred_element_type=jnp.float32
+        )
+
+    for part, (first, last) in enumerate(((0, 3), (3, 8), (8, steps))):
+        cols = slice(first * 2 * LANES, last * 2 * LANES)
         for u in range(first, last):
-            cols = slice(2 * u * LANES, 2 * (u + 1) * LANES)
-            q = factor[cols, :] * inv
-            qbuf[cols, :] = q
-            update = lax.dot_general(
-                o, q.astype(jnp.bfloat16), (((1,), (1,)), ((), ())), preferred_element_type=jnp.float32
-            )
-            dbuf[:, cols] = (scaling * update).astype(jnp.bfloat16)
-        cols = pl.ds(first * 2 * LANES, (last - first) * 2 * LANES)
-        for n, (src, dst) in enumerate(((dbuf.at[:, cols], direction.at[:, cols]), (qbuf.at[cols, :], qnew.at[cols, :]))):
-            copy = pltpu.make_async_copy(src, dst, sem.at[1 + part, n])
+            c = slice(2 * u * LANES, 2 * (u + 1) * LANES)
+            q = factor[c, :] * inv
+            qbuf[c, :] = q
+            dbuf[:, c] = (scaling * times(q)).astype(jnp.bfloat16)
+            mbuf[:, c] = (buf[:, c] - (1.0 - momentum_keep) * times(factor[c, :])).astype(jnp.bfloat16)
+        pairs = (
+            (qbuf.at[cols, :], qnew.at[cols, :]),
+            (dbuf.at[:, cols], direction.at[:, cols]),
+            (mbuf.at[:, cols], mout.at[:, cols]),
+        )
+        for n, (src, dst) in enumerate(pairs):
+            copy = pltpu.make_async_copy(src, dst, sem.at[part, n])
             copy.start()
             copies.append(copy)
     for copy in copies:
@@ -351,13 +362,13 @@
     dma = pltpu.SemaphoreType.DMA
     vmem = pl.BlockSpec(memory_space=pltpu.VMEM)
     hbm = pl.BlockSpec(memory_space=pltpu.HBM)
-    factor, ortho, sq, mnew = pl.pallas_call(
+    factor, ortho, sq, buffer = pl.pallas_call(
         main_kernel,
         out_shape=(
             jax.ShapeDtypeStruct((cols, LANES), f32),
             jax.ShapeDtypeStruct((rows, LANES), bf16),
             jax.ShapeDtypeStruct((8, LANES), f32),
-            jax.ShapeDtypeStruct((rows, cols), bf16),
+            jax.ShapeDtypeStruct((rows, cols), f32),
         ),
         in_specs=[hbm] * 3,
         out_specs=(vmem,) * 4,
@@ -365,7 +376,6 @@
             pltpu.VMEM((rows, cols), bf16),
             pltpu.VMEM((rows, cols), bf16),
             pltpu.VMEM((cols, LANES), f32),
-            pltpu.VMEM((rows, cols), f32),
             pltpu.VMEM((rows, cols), bf16),
             pltpu.VMEM((Z, rows // Z, LANES), f32),
             pltpu.VMEM((Z, rows // Z, LANES), f32),
@@ -384,7 +394,7 @@
             pltpu.VMEM((2 * CHIPS, -(-share // 16) * 16, LANES), bf16),
             pltpu.VMEM((2 * Z, 8, LANES), f32),
             pltpu.VMEM((CHIPS, 8, LANES), f32),
-            dma((4, 3)),
+            dma((5, 3)),
             dma((Z,)), dma((Z,)),
             dma((Z,)), dma((Z,)),
             dma, dma,
@@ -415,10 +425,15 @@
         ),
         in_specs=[vmem] * 4,
         out_specs=(hbm,) * 3,
-        scratch_shapes=[pltpu.VMEM((rows, cols), bf16), pltpu.VMEM((cols, LANES), f32), dma((4, 2))],
+        scratch_shapes=[
+            pltpu.VMEM((rows, cols), bf16),
+            pltpu.VMEM((rows, cols), bf16),
+            pltpu.VMEM((cols, LANES), f32),
+            dma((3, 3)),
+        ],
         compiler_params=pltpu.CompilerParams(vmem_limit_bytes=24 * 2**20),
         name="outputs",
-    )(factor, ortho, sq, mnew)
+    )(factor, ortho, sq, buffer)
 
 
 def solution(mesh):

time: 52.2 us -> 51.7 us (level)
    pallas_call x1, Pallas kernels: 49.2 us -> 48.3 us  [per_device(): pl.pallas_call(main_kernel, out_shape=(jax.ShapeDtypeStruct((cols, LANES)...]
where the time goes in v3:
time: 51.7 us; the launch traced here: 51.6 us
  Pallas kernels  51 us (99%)
  between operations  0.64 us (1%)
    pallas_call x1, Pallas kernels, per_device(): pl.pallas_call(main_kernel, out_shape=(jax.ShapeDtypeStruct((cols, LANES)...  48.3 us
    pallas_call x1, Pallas kernels, per_device(): pl.pallas_call(functools.partial(final_kernel, scaling), out_shape=(jax.S...  2.66 us

profile of v3, /device:TPU:1, one launch (start us, length us, event | category | flops | bytes accessed | tf_op | source)
XLA Modules:
  0.0 51.6 jit_solution(4806222902199991691)
XLA Ops:
  0.6 48.3 %power_gram_factor.1 = (f32[3328,128]{1,0:T(8,128)S(1)}, bf16[256,128]{1,0:T(8,128)(2,1)S(1)}, f32[8,128]{1,0:T(8,128)S(1)}, f32[256,3328]{1,0:T(8,128)S(1)}) custom-call(bf16[256,3328]{1,0:T(8,128)(2,1)} %grad.1, bf16[256,3328]{1,0:T(8,128)(2,1)} %mom.1, f32[3328,128]{1,0:T(8,128)} %qprev.1), custom_call_target="tpu_custom_call" | custom-call | tf_op jit(solution)/shard_map/power_gram_factor/pallas_call | solution.py:365
  49.0 2.7 %outputs.1 = (bf16[256,3328]{1,0:T(8,128)(2,1)}, bf16[256,3328]{1,0:T(8,128)(2,1)}, f32[3328,128]{1,0:T(8,128)}) custom-call(f32[3328,128]{1,0:T(8,128)S(1)} %get-tuple-element.7.factor, bf16[256,128]{1,0:T(8,128)(2,1)S(1)} %get-tuple-element.8.ortho, f32[8,128]{1,0:T(8,128)S(1)} %get-tuple-element.9.sq, f32[256,3328]{1,0:T(8,128)S(1)} %get-tuple-element.10.buf), custom_call_target="tpu_custom_call" | custom-call | tf_op jit(solution)/shard_map/outputs/pallas_call | solution.py:419

commit v4 on v3

--- a/solution.py
+++ b/solution.py
@@ -120,9 +120,9 @@
         pl.semaphore_signal(barrier, inc=1, device_id=dev, device_id_type=MESH)
     pl.semaphore_signal(barrier, inc=1, device_id=sibling, device_id_type=MESH)
 
-    bounds = [0, 8, 15, 21, tiles - 2, tiles]
+    bounds = [0, 7, 14, 20, tiles]
     loads = []
-    for i in range(5):
+    for i in range(4):
         lanes = pl.ds(bounds[i] * LANES, (bounds[i + 1] - bounds[i]) * LANES)
         part = [
             pltpu.make_async_copy(grad.at[:, lanes], gbuf.at[:, lanes], in_sem.at[i, 0]),
@@ -134,7 +134,7 @@
         loads.append(part)
 
     rows = bb.shape[0]
-    for i in range(5):
+    for i in range(4):
         for copy in loads[i]:
             copy.wait()
         lanes = pl.ds(bounds[i] * LANES, (bounds[i + 1] - bounds[i]) * LANES)
@@ -186,8 +186,7 @@
     hi = power.astype(jnp.bfloat16)
     p2[:, 0:128] = hi
     p2[:, 128:256] = (power - hi.astype(jnp.float32)).astype(jnp.bfloat16)
-    for i in range(5):
-        start, stop = bounds[i] * LANES, bounds[i + 1] * LANES
+    for start, stop in ((0, bb.shape[1] // 2), (bb.shape[1] // 2, bb.shape[1])):
         d = lax.dot_general(
             bb[:, start:stop], p2[...], (((0,), (0,)), ((), ())), preferred_element_type=jnp.float32
         )
@@ -270,9 +269,6 @@
     for s in range(1, CHIPS):
         w = w + wr[s]
     f = lax.dot_general(w, linv, (((1,), (1,)), ((), ())), precision=HIGHEST, preferred_element_type=jnp.float32)
-    sz[eight] = jnp.broadcast_to(jnp.sum(f * f, axis=0, keepdims=True), (8, LANES))
-    early, sends = sends, []
-    spread(sz, s9, r9, sends)
     fb[slot] = jnp.concatenate([f, jnp.zeros((fb.shape[1] - share, LANES), jnp.float32)], axis=0).astype(jnp.bfloat16)
     shared = []
     for i, (t, dev) in enumerate(f_others):
@@ -280,6 +276,9 @@
         copy.start()
         shared.append(copy)
 
+    sz[eight] = jnp.broadcast_to(jnp.sum(f * f, axis=0, keepdims=True), (8, LANES))
+    early, sends = sends, []
+    spread(sz, s9, r9, sends)
     def forward(t):
         place = t * 2 + k
         return remote(fb.at[place], fb.at[place], sf.at[t], r8.at[place], sibling)
@@ -334,7 +333,7 @@
             o, x.astype(jnp.bfloat16), (((1,), (1,)), ((), ())), preferred_element_type=jnp.float32
         )
 
-    for part, (first, last) in enumerate(((0, 3), (3, 8), (8, steps))):
+    for part, (first, last) in enumerate(((0, 1), (1, 4), (4, 8), (8, steps))):
         cols = slice(first * 2 * LANES, last * 2 * LANES)
         for u in range(first, last):
             c = slice(2 * u * LANES, 2 * (u + 1) * LANES)
@@ -394,7 +393,7 @@
             pltpu.VMEM((2 * CHIPS, -(-share // 16) * 16, LANES), bf16),
             pltpu.VMEM((2 * Z, 8, LANES), f32),
             pltpu.VMEM((CHIPS, 8, LANES), f32),
-            dma((5, 3)),
+            dma((4, 3)),
             dma((Z,)), dma((Z,)),
             dma((Z,)), dma((Z,)),
             dma, dma,
@@ -429,7 +428,7 @@
             pltpu.VMEM((rows, cols), bf16),
             pltpu.VMEM((rows, cols), bf16),
             pltpu.VMEM((cols, LANES), f32),
-            dma((3, 3)),
+            dma((4, 3)),
         ],
         compiler_params=pltpu.CompilerParams(vmem_limit_bytes=24 * 2**20),
         name="outputs",

time: 51.7 us -> 51.5 us (level)
  no operation moved by 1% of the time
where the time goes in v4:
time: 51.5 us; the launch traced here: 51.4 us
  Pallas kernels  50.8 us (99%)
  between operations  0.64 us (1%)
    pallas_call x1, Pallas kernels, per_device(): pl.pallas_call(main_kernel, out_shape=(jax.ShapeDtypeStruct((cols, LANES)...  48.1 us
    pallas_call x1, Pallas kernels, per_device(): pl.pallas_call(functools.partial(final_kernel, scaling), out_shape=(jax.S...  2.65 us

profile of v4, /device:TPU:1, one launch (start us, length us, event | category | flops | bytes accessed | tf_op | source)
XLA Modules:
  0.0 51.4 jit_solution(7546043070275702929)
XLA Ops:
  0.6 48.1 %power_gram_factor.1 = (f32[3328,128]{1,0:T(8,128)S(1)}, bf16[256,128]{1,0:T(8,128)(2,1)S(1)}, f32[8,128]{1,0:T(8,128)S(1)}, f32[256,3328]{1,0:T(8,128)S(1)}) custom-call(bf16[256,3328]{1,0:T(8,128)(2,1)} %grad.1, bf16[256,3328]{1,0:T(8,128)(2,1)} %mom.1, f32[3328,128]{1,0:T(8,128)} %qprev.1), custom_call_target="tpu_custom_call" | custom-call | tf_op jit(solution)/shard_map/power_gram_factor/pallas_call | solution.py:364
  48.8 2.6 %outputs.1 = (bf16[256,3328]{1,0:T(8,128)(2,1)}, bf16[256,3328]{1,0:T(8,128)(2,1)}, f32[3328,128]{1,0:T(8,128)}) custom-call(f32[3328,128]{1,0:T(8,128)S(1)} %get-tuple-element.7.factor, bf16[256,128]{1,0:T(8,128)(2,1)S(1)} %get-tuple-element.8.ortho, f32[8,128]{1,0:T(8,128)S(1)} %get-tuple-element.9.sq, f32[256,3328]{1,0:T(8,128)S(1)} %get-tuple-element.10.buf), custom_call_target="tpu_custom_call" | custom-call | tf_op jit(solution)/shard_map/outputs/pallas_call | solution.py:418

commit v5 on v3

--- a/solution.py
+++ b/solution.py
@@ -264,10 +264,9 @@
     linv = lmat[...]
 
     slot = chip * 2 + k
+    w = wr[chip]
     for s, _ in others:
         remote(wr.at[s], wr.at[s], s6.at[0], r6.at[s], sibling).wait_recv()
-    w = wr[0]
-    for s in range(1, CHIPS):
         w = w + wr[s]
     f = lax.dot_general(w, linv, (((1,), (1,)), ((), ())), precision=HIGHEST, preferred_element_type=jnp.float32)
     sz[eight] = jnp.broadcast_to(jnp.sum(f * f, axis=0, keepdims=True), (8, LANES))

time: 51.7 us -> 51.8 us (level)
  no operation moved by 1% of the time
where the time goes in v5:
time: 51.8 us; the launch traced here: 51.7 us
  Pallas kernels  51 us (98%)
  between operations  0.64 us (1%)
    pallas_call x1, Pallas kernels, per_device(): pl.pallas_call(main_kernel, out_shape=(jax.ShapeDtypeStruct((cols, LANES)...  48.4 us
    pallas_call x1, Pallas kernels, per_device(): pl.pallas_call(functools.partial(final_kernel, scaling), out_shape=(jax.S...  2.66 us

profile of v5, /device:TPU:1, one launch (start us, length us, event | category | flops | bytes accessed | tf_op | source)
XLA Modules:
  0.0 51.7 jit_solution(5590562722187799987)
XLA Ops:
  0.6 48.4 %power_gram_factor.1 = (f32[3328,128]{1,0:T(8,128)S(1)}, bf16[256,128]{1,0:T(8,128)(2,1)S(1)}, f32[8,128]{1,0:T(8,128)S(1)}, f32[256,3328]{1,0:T(8,128)S(1)}) custom-call(bf16[256,3328]{1,0:T(8,128)(2,1)} %grad.1, bf16[256,3328]{1,0:T(8,128)(2,1)} %mom.1, f32[3328,128]{1,0:T(8,128)} %qprev.1), custom_call_target="tpu_custom_call" | custom-call | tf_op jit(solution)/shard_map/power_gram_factor/pallas_call | solution.py:364
  49.0 2.7 %outputs.1 = (bf16[256,3328]{1,0:T(8,128)(2,1)}, bf16[256,3328]{1,0:T(8,128)(2,1)}, f32[3328,128]{1,0:T(8,128)}) custom-call(f32[3328,128]{1,0:T(8,128)S(1)} %get-tuple-element.7.factor, bf16[256,128]{1,0:T(8,128)(2,1)S(1)} %get-tuple-element.8.ortho, f32[8,128]{1,0:T(8,128)S(1)} %get-tuple-element.9.sq, f32[256,3328]{1,0:T(8,128)S(1)} %get-tuple-element.10.buf), custom_call_target="tpu_custom_call" | custom-call | tf_op jit(solution)/shard_map/outputs/pallas_call | solution.py:418
